TPU v7x, 128 devices: a whole 4x4x4 slice. The times are simulated.
128 devices in a mesh: lon: 16 (over x, y), lat: 8 (over z, core).
Axes of the slice: x: 4, y: 4, z: 4, core: 2. Of those that a mesh axis runs over, the one named last changes fastest.
Arguments:
- fields: float32 [4, 64, 1024, 128], P(None, 'lon', 'lat'), may hold values from -6 to 6
- mixing: float32 [4, 4, 128, 128], replicated
- classes: int32 [64, 1024], P('lon', 'lat'), may hold values from 0 to 15
Outputs:
- smoothed: float32 [4, 64, 1024, 128], P(None, 'lon', 'lat')
All inputs are finite; a program needn't handle non-finite values.
Results may differ from a plain program's by a relative error of at most 0.0003.
Values sent between devices are 32-bit elements; how exact they have to be, the bound alone decides.
A program may use at most 64 MiB of HBM per device.

v0:
```python
import jax
import jax.numpy as jnp
from jax import lax
from jax.sharding import PartitionSpec as P

smoothing_rate = 0.2
limit_scale = 2.0
substeps_per_turn = 4


def padded(cells, sides, width, closed):
    for axis, dim in sides:
        count = lax.axis_size(axis)
        ends = count if closed else count - 1
        head = lax.slice_in_dim(cells, 0, width, axis=dim)
        tail = lax.slice_in_dim(cells, cells.shape[dim] - width, cells.shape[dim], axis=dim)
        cells = jnp.concatenate(
            [
                lax.ppermute(tail, axis, [(i, (i + 1) % count) for i in range(ends)]),
                cells,
                lax.ppermute(head, axis, [((i + 1) % count, i) for i in range(ends)]),
            ],
            axis=dim,
        )
    return cells


def chain(values, mixing):
    for operator_index in range(mixing.shape[1]):
        mixed = jnp.einsum(
            "fcb,fab->fca", values, mixing[:, operator_index], precision=lax.Precision.HIGHEST
        )
        values = limit_scale * jnp.tanh(mixed / limit_scale)
    return values


def advance(column_data, step_counts, mixing):
    column_count = column_data.shape[1]
    group_size = 512
    ordering = jnp.argsort(step_counts, stable=True)
    inverse = jnp.argsort(ordering, stable=True)
    ordered = jnp.take(column_data, ordering, axis=1)
    ordered_steps = jnp.take(step_counts, ordering, axis=0)

    def one_group(group_index, current):
        block_data = current

        def several_substeps(outer_index, values):
            for inner_index in range(substeps_per_turn):
                turn_index = outer_index * substeps_per_turn + inner_index
                updated = chain(values, mixing)
                values = jnp.where((turn_index < ordered_steps)[None, :, None], updated, values)
            return values

        turn_count = (ordered_steps[group_size - 1] + substeps_per_turn - 1) // substeps_per_turn
        block_data = lax.fori_loop(0, turn_count, several_substeps, block_data)
        return block_data

    result = lax.fori_loop(0, column_count // group_size, one_group, ordered)
    return jnp.take(result, inverse, axis=1)


def per_device(fields, mixing, classes):
    field_count, lon_cells, lat_cells, levels = fields.shape
    column_total = lon_cells * lat_cells
    column_data = fields.reshape(field_count, column_total, levels)
    step_counts = (classes + 1).reshape(column_total)
    lon_devices = lax.axis_size("lon")
    lat_devices = lax.axis_size("lat")
    all_devices = lon_devices * lat_devices
    piece_cols = column_total // all_devices
    outgoing = column_data.reshape(field_count, all_devices, piece_cols, levels)
    outgoing_steps = step_counts.reshape(1, all_devices, piece_cols)
    values = lax.all_to_all(outgoing, ("lon", "lat"), split_axis=1, concat_axis=1, tiled=True)
    owned_steps = lax.all_to_all(
        outgoing_steps, ("lon", "lat"), split_axis=1, concat_axis=1, tiled=True
    )
    items = values.shape[2]
    flattened = values.reshape(field_count, all_devices * items, levels)
    advanced = advance(flattened, owned_steps.reshape(all_devices * items), mixing)
    advanced = advanced.reshape(field_count, all_devices, items, levels)
    returned = lax.all_to_all(advanced, ("lon", "lat"), split_axis=1, concat_axis=1, tiled=True)
    column_state = returned.reshape(field_count, lon_cells, lat_cells, levels)
    lon_padded = padded(column_state, (("lon", 1),), 1, True)
    lat_padded = padded(column_state, (("lat", 2),), 1, False)
    lat_position = jnp.arange(lat_cells)
    low_edge = (lat_position == 0) & (lax.axis_index("lat") == 0)
    high_edge = (lat_position == lat_cells - 1) & (lax.axis_index("lat") == lat_devices - 1)
    southern = jnp.where(low_edge[None, None, :, None], column_state, lat_padded[:, :, :-2])
    northern = jnp.where(high_edge[None, None, :, None], column_state, lat_padded[:, :, 2:])
    eastern = lon_padded[:, 2:]
    western = lon_padded[:, :-2]
    return column_state + smoothing_rate * (
        eastern + western + northern + southern - 4.0 * column_state
    )


def solution(mesh):
    in_specs = (P(None, "lon", "lat", None), P(), P("lon", "lat"))
    out_specs = P(None, "lon", "lat", None)
    return jax.shard_map(
        per_device, mesh=mesh, in_specs=in_specs, out_specs=out_specs, check_vma=False
    )
```

profile of v0, /device:TPU:1, one launch (start us, length us, event | category | flops | bytes accessed | tf_op | source)
XLA Modules:
  0.0 164.1 jit_solution(1921666592057640069)
XLA Ops:
  1.4 11.5 %all-to-all-start.1 = ((s32[1,128,4]{2,0,1:T(1,128)}), s32[1,128,4]{2,0,1:T(1,128)S(1)}, u32[]{:S(2)}, u32[]{:S(2)}) async-start(s32[1,128,4]{2,0,1:T(1,128)} %bitcast.4), calls=%async_computation.1 | async-start | bytes 131072 | tf_op jit(solution)/shard_map/all_to_all | solution.py:75
  12.9 3.0 %copy.11 = f32[4,128,4,128]{3,0,2,1:T(4,128)} copy(f32[4,128,4,128]{3,2,1,0:T(4,128)} %bitcast.131) | data formatting | bytes 2097152 | tf_op jit(solution)/shard_map/reshape;reshape | solution.py:72
  16.0 6.3 %all-to-all-done.1 = s32[1,128,4]{2,0,1:T(1,128)S(1)} async-done(((s32[1,128,4]{2,0,1:T(1,128)}), s32[1,128,4]{2,0,1:T(1,128)S(1)}, u32[]{:S(2)}, u32[]{:S(2)}) %all-to-all-start.1) | async-done | bytes 2080 | tf_op jit(solution)/shard_map/all_to_all | solution.py:75
  22.3 4.8 %all-to-all-start = ((f32[4,128,4,128]{3,0,2,1:T(4,128)}), f32[4,128,4,128]{3,0,2,1:T(4,128)S(1)}, u32[]{:S(2)}, u32[]{:S(2)}) async-start(f32[4,128,4,128]{3,0,2,1:T(4,128)} %copy.11), calls=%async_computation | async-start | bytes 2097152 | tf_op jit(solution)/shard_map/all_to_all | solution.py:74
  28.6 3.8 %sort.31 = (s32[512]{0:T(512)}, s32[512]{0:T(512)S(1)}) sort(s32[512]{0:T(512)S(1)} %reshape.47, s32[512]{0:T(512)S(1)} %iota.16), dimensions={0}, to_apply=%region_0.0 | sort | flops 4608 | bytes 8192 | tf_op jit(solution)/shard_map/jit(argsort)/sort | solution.py:40
  32.4 3.5 %gather_fusion = s32[512]{0:T(512)S(1)} fusion(s32[512]{0:T(512)S(1)} %reshape.47, s32[1024]{0:T(1024)S(1)} %pad_clamp_fusion.1), kind=kCustom, calls=%fused_computation.2 | custom fusion | bytes 6144 | tf_op jit(solution)/shard_map/jit(_take)/gather | solution.py:43
  37.3 3.8 %sort.32 = (s32[512]{0:T(512)}, s32[512]{0:T(512)S(1)}) sort(s32[512]{0:T(512)S(1)} %get-tuple-element.48, s32[512]{0:T(512)S(1)} %iota.17), dimensions={0}, to_apply=%region_3.5 | sort | flops 4608 | bytes 8192 | tf_op jit(solution)/shard_map/jit(argsort)/sort | solution.py:41
  41.1 5.2 %all-to-all-done = f32[4,128,4,128]{3,0,2,1:T(4,128)S(1)} async-done(((f32[4,128,4,128]{3,0,2,1:T(4,128)}), f32[4,128,4,128]{3,0,2,1:T(4,128)S(1)}, u32[]{:S(2)}, u32[]{:S(2)}) %all-to-all-start) | async-done | bytes 1048608 | tf_op jit(solution)/shard_map/all_to_all | solution.py:74
  46.3 2.1 %gather_fusion.1 = f32[512,4,128]{2,1,0:T(4,128)S(1)} fusion(f32[4,512,128]{2,0,1:T(4,128)S(1)} %bitcast.130, s32[1024]{0:T(1024)S(1)} %pad_clamp_fusion.1), kind=kCustom, calls=%fused_computation.clone | custom fusion | bytes 2099200 | tf_op jit(solution)/shard_map/jit(_take)/gather | solution.py:42
  48.4 1.8 %select_bitcast_fusion = f32[4,512,128]{2,0,1:T(4,128)S(1)} fusion(f32[512,4,128]{2,1,0:T(4,128)S(1)} %gather_fusion.1, pred[512]{0:T(512)(128)(4,1)S(1)} %get-tuple-element.77), kind=kLoop, calls=%fused_computation.103 | loop fusion | flops 262144 | bytes 2097664 | tf_op jit(solution)/shard_map/jit(_take)/select_n | solution.py:42
  50.2 71.3 %while.17 = (s32[]{:T(128)}, f32[4,512,128]{2,1,0:T(8,128)S(1)}, s32[]{:T(128)}, s32[512]{0:T(512)S(1)}, f32[4,4,128,128]{3,2,0,1:T(8,128)S(1)}, /*index=5*/s32[]{:T(128)}, s32[]{:T(128)}, s32[]{:T(128)}, s32[]{:T(128)}) while((s32[]{:T(128)}, f32[4,512,128]{2,1,0:T(8,128)S(1)}, s32[]{:T(128)}, s32[512]{0:T(512)S(1)}, ...), condition=%wide.region_2.4_spmd, body=%wide.region_1.3_spmd.sunk | while | flops 6451890176 | bytes 41949340 | solution.py:56
  53.8 1.2 fusion.177
  71.5 1.2 fusion.177
  89.2 1.2 fusion.177
  107.0 1.2 fusion.177
  122.3 2.1 %gather_fusion.2 = f32[512,4,128]{2,1,0:T(4,128)S(1)} fusion(f32[4,512,128]{2,0,1:T(4,128)S(1)} %copy.14, s32[1024]{0:T(1024)S(1)} %pad_clamp_fusion), kind=kCustom, calls=%fused_computation.1.clone | custom fusion | bytes 2099200 | tf_op jit(solution)/shard_map/jit(_take)/gather | solution.py:60
  124.4 2.6 %broadcast_select_fusion = f32[512,4,128]{2,1,0:T(4,128)} fusion(f32[512,4,128]{2,1,0:T(4,128)S(1)} %gather_fusion.2, pred[512]{0:T(512)(128)(4,1)S(1)} %compare_and_fusion), kind=kLoop, calls=%fused_computation.104 | loop fusion | flops 262144 | bytes 2097664 | tf_op jit(solution)/shard_map/jit(_take)/select_n | solution.py:60
  127.0 4.6 %all-to-all-start.2 = ((f32[4,128,4,128]{3,0,2,1:T(4,128)}), f32[4,128,4,128]{3,0,2,1:T(4,128)S(1)}, u32[]{:S(2)}, u32[]{:S(2)}) async-start(f32[4,128,4,128]{3,0,2,1:T(4,128)} %bitcast.10), calls=%async_computation.2 | async-start | bytes 2097152 | tf_op jit(solution)/shard_map/all_to_all | solution.py:82
  131.6 19.4 %all-to-all-done.2 = f32[4,128,4,128]{3,0,2,1:T(4,128)S(1)} async-done(((f32[4,128,4,128]{3,0,2,1:T(4,128)}), f32[4,128,4,128]{3,0,2,1:T(4,128)S(1)}, u32[]{:S(2)}, u32[]{:S(2)}) %all-to-all-start.2) | async-done | bytes 1048608 | tf_op jit(solution)/shard_map/all_to_all | solution.py:82
  151.3 1.2 collective-permute-start
  152.9 3.6 %collective-permute-start.2 = (f32[4,4,1,128]{3,2,1,0:T(1,128)S(1)}, f32[4,4,1,128]{3,2,1,0:T(1,128)S(1)}, u32[]{:S(2)}, u32[]{:S(2)}) collective-permute-start(f32[4,4,1,128]{3,2,1,0:T(1,128)S(1)} %get-tuple-element.84), channel_id=1, source_target_pairs={{1,0},{2,1},{3,2},{4,3},{5,4},{6,5},{7,6},{9,8},{10,9},{11,10},{12... | collective-permute-start | bytes 24584 | tf_op jit(solution)/shard_map/ppermute | solution.py:21
  156.5 1.9 %collective-permute-start.3 = (f32[4,4,1,128]{3,2,1,0:T(1,128)S(1)}, f32[4,4,1,128]{3,2,1,0:T(1,128)S(1)}, u32[]{:S(2)}, u32[]{:S(2)}) collective-permute-start(f32[4,4,1,128]{3,2,1,0:T(1,128)S(1)} %get-tuple-element.85), channel_id=1, source_target_pairs={{0,1},{1,2},{2,3},{3,4},{4,5},{5,6},{6,7},{8,9},{9,10},{10,11},{11... | collective-permute-start | bytes 24584 | tf_op jit(solution)/shard_map/ppermute | solution.py:19
  159.6 3.0 %collective-permute-done.1 = f32[4,1,128,128]{3,2,1,0:T(8,128)S(1)} collective-permute-done((f32[4,1,128,128]{3,2,1,0:T(8,128)S(1)}, f32[4,1,128,128]{3,2,1,0:T(8,128)S(1)}, u32[]{:S(2)}, u32[]{:S(2)}) %collective-permute-start.1) | collective-permute-done | bytes 262176 | tf_op jit(solution)/shard_map/ppermute | solution.py:19
  162.6 1.6 fusion.72
  (91 shorter events, 71.9 us)
Async XLA Ops:
  1.4 20.9 %all-to-all-start.1 = ((s32[1,128,4]{2,0,1:T(1,128)}), s32[1,128,4]{2,0,1:T(1,128)S(1)}, u32[]{:S(2)}, u32[]{:S(2)}) async-start(s32[1,128,4]{2,0,1:T(1,128)} %bitcast.4), calls=%async_computation.1 | async-start | bytes 131072 | tf_op jit(solution)/shard_map/all_to_all | solution.py:75
  12.9 3.0 %copy-start = (f32[4,4,128,128]{3,2,1,0:T(8,128)S(1)}, f32[4,4,128,128]{3,2,1,0:T(8,128)}, u32[]{:S(2)}) copy-start(f32[4,4,128,128]{3,2,1,0:T(8,128)} %param.8) | copy-start | bytes 3145732
  22.3 24.1 %all-to-all-start = ((f32[4,128,4,128]{3,0,2,1:T(4,128)}), f32[4,128,4,128]{3,0,2,1:T(4,128)S(1)}, u32[]{:S(2)}, u32[]{:S(2)}) async-start(f32[4,128,4,128]{3,0,2,1:T(4,128)} %copy.11), calls=%async_computation | async-start | bytes 2097152 | tf_op jit(solution)/shard_map/all_to_all | solution.py:74
  127.0 24.0 %all-to-all-start.2 = ((f32[4,128,4,128]{3,0,2,1:T(4,128)}), f32[4,128,4,128]{3,0,2,1:T(4,128)S(1)}, u32[]{:S(2)}, u32[]{:S(2)}) async-start(f32[4,128,4,128]{3,0,2,1:T(4,128)} %bitcast.10), calls=%async_computation.2 | async-start | bytes 2097152 | tf_op jit(solution)/shard_map/all_to_all | solution.py:82
  151.3 8.3 %collective-permute-start = (f32[4,1,128,128]{3,2,1,0:T(8,128)S(1)}, f32[4,1,128,128]{3,2,1,0:T(8,128)S(1)}, u32[]{:S(2)}, u32[]{:S(2)}) collective-permute-start(f32[4,1,128,128]{3,2,1,0:T(8,128)S(1)} %get-tuple-element.82), channel_id=1, source_target_pairs={{8,0},{16,8},{24,16},{32,24},{40,32},{48,40},{56,48},{64,56},{72,6... | collective-permute-start | bytes 786440 | tf_op jit(solution)/shard_map/ppermute | solution.py:21
  152.6 10.0 %collective-permute-start.1 = (f32[4,1,128,128]{3,2,1,0:T(8,128)S(1)}, f32[4,1,128,128]{3,2,1,0:T(8,128)S(1)}, u32[]{:S(2)}, u32[]{:S(2)}) collective-permute-start(f32[4,1,128,128]{3,2,1,0:T(8,128)S(1)} %get-tuple-element.83), channel_id=1, source_target_pairs={{0,8},{8,16},{16,24},{24,32},{32,40},{40,48},{48,56},{56,64},{64,7... | collective-permute-start | bytes 786440 | tf_op jit(solution)/shard_map/ppermute | solution.py:19
  152.9 5.6 %collective-permute-start.2 = (f32[4,4,1,128]{3,2,1,0:T(1,128)S(1)}, f32[4,4,1,128]{3,2,1,0:T(1,128)S(1)}, u32[]{:S(2)}, u32[]{:S(2)}) collective-permute-start(f32[4,4,1,128]{3,2,1,0:T(1,128)S(1)} %get-tuple-element.84), channel_id=1, source_target_pairs={{1,0},{2,1},{3,2},{4,3},{5,4},{6,5},{7,6},{9,8},{10,9},{11,10},{12... | collective-permute-start | bytes 24584 | tf_op jit(solution)/shard_map/ppermute | solution.py:21
  156.5 3.1 %collective-permute-start.3 = (f32[4,4,1,128]{3,2,1,0:T(1,128)S(1)}, f32[4,4,1,128]{3,2,1,0:T(1,128)S(1)}, u32[]{:S(2)}, u32[]{:S(2)}) collective-permute-start(f32[4,4,1,128]{3,2,1,0:T(1,128)S(1)} %get-tuple-element.85), channel_id=1, source_target_pairs={{0,1},{1,2},{2,3},{3,4},{4,5},{5,6},{6,7},{8,9},{9,10},{10,11},{11... | collective-permute-start | bytes 24584 | tf_op jit(solution)/shard_map/ppermute | solution.py:19
where the time goes:
time: 165 us; the launch traced here: 164 us
  matrix products  70.3 us (43%)
  waiting for transfers between devices  35 us (21%)
  starting transfers between devices  27.9 us (17%)
  other arithmetic  15.1 us (9%)
  local copies, waits for them, and re-layouts  13.8 us (8%)
    dot_general x64, matrix products, chain(): jnp.einsum('fcb,fab->fca', values, mixing[:, operator_index], precision=l...  70.3 us
    all_to_all x1, waiting for transfers between devices, per_device(): lax.all_to_all(advanced, ('lon', 'lat'), split_axis=1, concat_axis=1, til...  19.4 us
    all_to_all x1, starting transfers between devices, per_device(): lax.all_to_all(outgoing_steps, ('lon', 'lat'), split_axis=1, concat_axis=...  11.5 us
    all_to_all x1, waiting for transfers between devices, per_device(): lax.all_to_all(outgoing_steps, ('lon', 'lat'), split_axis=1, concat_axis=...  6.29 us
    all_to_all x1, waiting for transfers between devices, per_device(): lax.all_to_all(outgoing, ('lon', 'lat'), split_axis=1, concat_axis=1, til...  5.22 us
    ppermute x2, starting transfers between devices, padded(): lax.ppermute(head, axis, [((i + 1) % count, i) for i in range(ends)])  4.88 us
    all_to_all x1, starting transfers between devices, per_device(): lax.all_to_all(outgoing, ('lon', 'lat'), split_axis=1, concat_axis=1, til...  4.76 us
    all_to_all x1, starting transfers between devices, per_device(): lax.all_to_all(advanced, ('lon', 'lat'), split_axis=1, concat_axis=1, til...  4.6 us
  transfers between devices with their start and end apart: 7, of which 5 were waited for; matrix products, arithmetic and copies ran while one was open for 10% of the time, Pallas kernels for 0%

commit v1 on v0

v1 whole, which is shorter than its diff:
```python
import functools

import jax
import jax.numpy as jnp
from jax import lax
from jax.experimental import pallas as pl
from jax.experimental.pallas import tpu as pltpu
from jax.sharding import PartitionSpec as P

STEPS = 16
UNROLL = 4
PAD = 16
MESH = pl.DeviceIdType.MESH


def split(values):
    high = values.astype(jnp.bfloat16)
    low = (values - high.astype(jnp.float32)).astype(jnp.bfloat16)
    return high, low


def advance(state, limits, weights):
    field_count, ops = weights.shape[0], weights.shape[1]

    def substeps(turn, _):
        current = [state[f] for f in range(field_count)]
        for k in range(UNROLL):
            active = limits[...] > turn * UNROLL + k
            values = list(current)
            for o in range(ops):
                for f in range(field_count):
                    pieces = jnp.concatenate(split(values[f]), axis=1)
                    mixed = jnp.dot(pieces, weights[f, o], preferred_element_type=jnp.float32)
                    half = mixed.shape[1] // 2
                    values[f] = jnp.tanh(mixed[:, :half] + mixed[:, half:])
            current = [jnp.where(active, new, old) for new, old in zip(values, current)]
        for f in range(field_count):
            state[f] = current[f]
        return 0

    lax.fori_loop(0, STEPS // UNROLL, substeps, 0)


def kernel(
    fields, mixing, classes, out,
    outer, inner, outer_limits, inner_limits, matrices, weights,
    north_send, south_send, east_halo, west_halo, north_halo, south_halo, result,
    load_sem, mix_sem, send_sem, recv_sem, out_sem,
):
    field_count, lons, lats, levels = fields.shape
    ops = mixing.shape[1]
    lon, lat = lax.axis_index("lon"), lax.axis_index("lat")
    lon_count, lat_count = lax.axis_size("lon"), lax.axis_size("lat")
    east = (lax.rem(lon + 1, lon_count), lat)
    west = (lax.rem(lon + lon_count - 1, lon_count), lat)
    north = (lon, lax.rem(lat + 1, lat_count))
    south = (lon, lax.rem(lat + lat_count - 1, lat_count))

    mix_copy = pltpu.make_async_copy(mixing, matrices, mix_sem)
    mix_copy.start()
    places = [(outer, 0), (inner, 0), (inner, lats), (outer, lats)]
    loads = []
    for f in range(field_count):
        for i in range(lons):
            buffer, row = places[i]
            copy = pltpu.make_async_copy(
                fields.at[f, i], buffer.at[f, pl.ds(row, lats)], load_sem.at[f * lons + i]
            )
            copy.start()
            loads.append(copy)

    barrier = pltpu.get_barrier_semaphore()
    for neighbour in (east, west, north, south):
        pl.semaphore_signal(barrier, inc=1, device_id=neighbour, device_id_type=MESH)

    edge_rows = []
    for i in range(lons):
        buffer, row = (outer_limits, places[i][1]) if i in (0, lons - 1) else (inner_limits, places[i][1])
        limit = jnp.broadcast_to(classes[pl.ds(i, 1), :] + 1, (levels, lats)).T
        buffer[pl.ds(row, lats), :] = limit
        if i in (1, 2):
            edge_rows += [limit[:1], limit[lats - 1:]]
    outer_limits[pl.ds(2 * lats, PAD), :] = jnp.concatenate(
        edge_rows + [jnp.zeros((PAD - 4, levels), jnp.int32)], axis=0
    )

    mix_copy.wait()
    for f in range(field_count):
        for o in range(ops):
            pieces = jnp.concatenate(split(matrices[f, o]), axis=0).T
            weights[f, o, pl.ds(0, levels), :] = pieces
            weights[f, o, pl.ds(levels, levels), :] = pieces

    for copy in loads:
        copy.wait()
    for f in range(field_count):
        outer[f, pl.ds(0, 2 * lats), :] = 0.5 * outer[f, pl.ds(0, 2 * lats), :]
        inner[f] = 0.5 * inner[f]
        outer[f, pl.ds(2 * lats, PAD), :] = jnp.concatenate(
            [
                inner[f, pl.ds(0, 1), :],
                inner[f, pl.ds(lats - 1, 1), :],
                inner[f, pl.ds(lats, 1), :],
                inner[f, pl.ds(2 * lats - 1, 1), :],
                jnp.zeros((PAD - 4, levels), jnp.float32),
            ],
            axis=0,
        )

    advance(outer, outer_limits, weights)

    low_rows = (0, 2 * lats, 2 * lats + 2, lats)
    high_rows = (lats - 1, 2 * lats + 1, 2 * lats + 3, 2 * lats - 1)
    for f in range(field_count):
        for i in range(lons):
            south_send[pl.ds(f * lons + i, 1), :] = outer[f, pl.ds(low_rows[i], 1), :]
            north_send[pl.ds(f * lons + i, 1), :] = outer[f, pl.ds(high_rows[i], 1), :]

    pl.semaphore_wait(barrier, 4)
    copies = []

    def send(source, target, device):
        slot = len(copies)
        copy = pltpu.make_async_remote_copy(
            src_ref=source, dst_ref=target, send_sem=send_sem.at[slot], recv_sem=recv_sem.at[slot],
            device_id=device, device_id_type=MESH,
        )
        copy.start()
        copies.append(copy)

    send(north_send, south_halo, north)
    send(south_send, north_halo, south)
    for f in range(field_count):
        send(outer.at[f, pl.ds(lats, lats)], west_halo.at[f], east)
        send(outer.at[f, pl.ds(0, lats)], east_halo.at[f], west)

    advance(inner, inner_limits, weights)

    for copy in copies:
        copy.wait()

    row = lax.broadcasted_iota(jnp.int32, (lats, levels), 0)
    stores = []
    for f in range(field_count):
        cells = [
            outer[f, pl.ds(0, lats), :],
            inner[f, pl.ds(0, lats), :],
            inner[f, pl.ds(lats, lats), :],
            outer[f, pl.ds(lats, lats), :],
        ]
        around = [west_halo[f]] + cells + [east_halo[f]]
        for i in range(lons):
            cell = cells[i]
            k = f * lons + i
            above = jnp.where(lat == lat_count - 1, cell[lats - 1:], north_halo[pl.ds(k, 1), :])
            below = jnp.where(lat == 0, cell[:1], south_halo[pl.ds(k, 1), :])
            northern = jnp.where(row == lats - 1, above, pltpu.roll(cell, lats - 1, 0))
            southern = jnp.where(row == 0, below, pltpu.roll(cell, 1, 0))
            result[f, i] = 0.4 * (cell + around[i] + around[i + 2] + northern + southern)
        copy = pltpu.make_async_copy(result.at[f], out.at[f], out_sem.at[f])
        copy.start()
        stores.append(copy)
    for copy in stores:
        copy.wait()


def per_device(fields, mixing, classes):
    field_count, lons, lats, levels = fields.shape
    ops = mixing.shape[1]
    f32, i32 = jnp.float32, jnp.int32
    halo = pltpu.VMEM((field_count, lats, levels), f32)
    edge = pltpu.VMEM((field_count * lons, levels), f32)
    copies = 2 + 2 * field_count
    rows = STEPS * ops * field_count * (lons * lats + PAD)
    return pl.pallas_call(
        kernel,
        out_shape=jax.ShapeDtypeStruct(fields.shape, f32),
        in_specs=[
            pl.BlockSpec(memory_space=pl.ANY),
            pl.BlockSpec(memory_space=pl.ANY),
            pl.BlockSpec(memory_space=pltpu.VMEM),
        ],
        out_specs=pl.BlockSpec(memory_space=pl.ANY),
        scratch_shapes=[
            pltpu.VMEM((field_count, 2 * lats + PAD, levels), f32),
            pltpu.VMEM((field_count, 2 * lats, levels), f32),
            pltpu.VMEM((2 * lats + PAD, levels), i32),
            pltpu.VMEM((2 * lats, levels), i32),
            pltpu.VMEM(mixing.shape, f32),
            pltpu.VMEM((field_count, ops, 2 * levels, 2 * levels), jnp.bfloat16),
            edge, edge, halo, halo, edge, edge,
            pltpu.VMEM(fields.shape, f32),
            pltpu.SemaphoreType.DMA((field_count * lons,)),
            pltpu.SemaphoreType.DMA,
            pltpu.SemaphoreType.DMA((copies,)),
            pltpu.SemaphoreType.DMA((copies,)),
            pltpu.SemaphoreType.DMA((field_count,)),
        ],
        compiler_params=pltpu.CompilerParams(
            collective_id=0, has_side_effects=True, vmem_limit_bytes=40 * 2**20
        ),
        cost_estimate=pl.CostEstimate(
            flops=2 * rows * (2 * levels) ** 2, bytes_accessed=12 * 2**20 // 4, transcendentals=rows * levels
        ),
    )(fields, mixing, classes)


def solution(mesh):
    in_specs = (P(None, "lon", "lat", None), P(), P("lon", "lat"))
    out_specs = P(None, "lon", "lat", None)
    return jax.shard_map(
        per_device, mesh=mesh, in_specs=in_specs, out_specs=out_specs, check_vma=False
    )
```

time: 165 us -> 28.9 us (0.18)
  matrix products: 70.3 us -> 0 us
  waiting for transfers between devices: 35 us -> 0 us
  starting transfers between devices: 27.9 us -> 0 us
  Pallas kernels: 0 us -> 24.6 us
  other arithmetic: 15.1 us -> 0 us
  local copies, waits for them, and re-layouts: 13.8 us -> 4.1 us
    dot_general x64 -> x0, matrix products: 70.3 us -> none  [chain(): jnp.einsum('fcb,fab->fca', values, mixing[:, operator_index], precision=l...]
    all_to_all x3 -> x0, waiting for transfers between devices: 30.9 us -> none  [the longest x1 19.4 us: per_device(): lax.all_to_all(advanced, ('lon', 'lat'), split_axis=1, concat_axis=1, til...]
    pallas_call x0 -> x1, Pallas kernels: none -> 24.6 us  [per_device(): pl.pallas_call(kernel, out_shape=jax.ShapeDtypeStruct(fields.shape, f32),...]
    all_to_all x3 -> x0, starting transfers between devices: 20.8 us -> none  [the longest x1 11.5 us: per_device(): lax.all_to_all(outgoing_steps, ('lon', 'lat'), split_axis=1, concat_axis=...]
    gather x3 -> x0, local copies, waits for them, and re-layouts: 7.64 us -> none  [the longest x1 3.49 us: advance(): ordered_steps = jnp.take(step_counts, ordering, axis=0)]
    sort x2 -> x0, other arithmetic: 7.57 us -> none  [the longest x1 3.78 us: advance(): ordering = jnp.argsort(step_counts, stable=True)]
    ppermute x4 -> x0, starting transfers between devices: 7.1 us -> none  [the longest x2 4.88 us: padded(): lax.ppermute(head, axis, [((i + 1) % count, i) for i in range(ends)])]
    select_n x5 -> x0, other arithmetic: 4.39 us -> none  [the longest x2 2.63 us: advance(): return jnp.take(result, inverse, axis=1)]
  transfers between devices with their start and end apart: 7 -> 0, of which waited for: 5 -> 0; matrix products, arithmetic and copies ran while one was open for 10% -> 0% of each run, Pallas kernels for 0% -> 0%
where the time goes in v1:
time: 28.9 us; the launch traced here: 28.7 us
  Pallas kernels  24.6 us (85%)
  local copies, waits for them, and re-layouts  4.1 us (14%)
    pallas_call x1, Pallas kernels, per_device(): pl.pallas_call(kernel, out_shape=jax.ShapeDtypeStruct(fields.shape, f32),...  24.6 us
    unnamed x7, local copies, waits for them, and re-layouts  4.1 us

profile of v1, /device:TPU:1, one launch (start us, length us, event | category | flops | bytes accessed | tf_op | source)
XLA Modules:
  0.0 28.7 jit_solution(6340343031729016515)
XLA Ops:
  0.0 0.0 copy-start
  0.0 1.2 %copy-done = f32[4,4,128,128]{3,2,1,0:T(8,128)S(1)} copy-done((f32[4,4,128,128]{3,2,1,0:T(8,128)S(1)}, f32[4,4,128,128]{3,2,1,0:T(8,128)}, u32[]{:S(2)}) %copy-start) | copy-done | bytes 1048600
  1.2 0.0 copy-start.1
  1.2 1.2 %copy-done.1 = f32[4,4,128,128]{3,2,1,0:T(8,128)S(1)} copy-done((f32[4,4,128,128]{3,2,1,0:T(8,128)S(1)}, f32[4,4,128,128]{3,2,1,0:T(8,128)}, u32[]{:S(2)}) %copy-start.1) | copy-done | bytes 1048600
  2.5 0.0 copy-start.2
  2.5 0.7 %copy-done.2 = s32[4,128]{1,0:T(4,128)S(1)} copy-done((s32[4,128]{1,0:T(4,128)S(1)}, s32[4,128]{1,0:T(4,128)}, u32[]{:S(2)}) %copy-start.2) | copy-done | bytes 2072
  3.1 24.6 %shard_map.37 = f32[4,4,128,128]{3,2,1,0:T(8,128)S(1)} custom-call(f32[4,4,128,128]{3,2,1,0:T(8,128)S(1)} %copy-done, f32[4,4,128,128]{3,2,1,0:T(8,128)S(1)} %copy-done.1, s32[4,128]{1,0:T(4,128)S(1)} %copy-done.2), custom_call_target="tpu_custom_call" | custom-call | flops 17716740096 | bytes 3145728 | tf_op jit(solution)/shard_map/pallas_call | solution.py:175
  27.8 1.0 %copy.5 = f32[4,4,128,128]{3,2,1,0:T(8,128)} copy(f32[4,4,128,128]{3,2,1,0:T(8,128)S(1)} %shard_map.37) | data formatting | bytes 2097152
Async XLA Ops:
  0.0 1.2 %copy-start = (f32[4,4,128,128]{3,2,1,0:T(8,128)S(1)}, f32[4,4,128,128]{3,2,1,0:T(8,128)}, u32[]{:S(2)}) copy-start(f32[4,4,128,128]{3,2,1,0:T(8,128)} %fields.1) | copy-start | bytes 3145732
  1.2 1.2 %copy-start.1 = (f32[4,4,128,128]{3,2,1,0:T(8,128)S(1)}, f32[4,4,128,128]{3,2,1,0:T(8,128)}, u32[]{:S(2)}) copy-start(f32[4,4,128,128]{3,2,1,0:T(8,128)} %mixing.1) | copy-start | bytes 3145732
  2.5 0.7 %copy-start.2 = (s32[4,128]{1,0:T(4,128)S(1)}, s32[4,128]{1,0:T(4,128)}, u32[]{:S(2)}) copy-start(s32[4,128]{1,0:T(4,128)} %classes.1) | copy-start | bytes 6148

commit v2 on v1

v2 whole, which is shorter than its diff:
```python
import functools

import jax
import jax.numpy as jnp
from jax import lax
from jax.experimental import pallas as pl
from jax.experimental.pallas import tpu as pltpu
from jax.sharding import PartitionSpec as P

STEPS = 16
HEAD = 4
PAD = 16
MESH = pl.DeviceIdType.MESH


def split(values):
    high = values.astype(jnp.bfloat16)
    low = (values - high.astype(jnp.float32)).astype(jnp.bfloat16)
    return high, low


def advance(units, count, weights):
    current = [state[f] for state, _, f, _ in units]
    for _ in range(count):
        values = list(current)
        for o in range(weights.shape[1]):
            for k, (_, _, f, _) in enumerate(units):
                pieces = jnp.concatenate(split(values[k]), axis=1)
                mixed = jnp.dot(pieces, weights[f, o], preferred_element_type=jnp.float32)
                half = mixed.shape[1] // 2
                values[k] = jnp.tanh(mixed[:, :half] + mixed[:, half:])
        for k, unit in enumerate(units):
            current[k] = jnp.where(unit[1][...] > unit[3], values[k], current[k])
            unit[3] += 1
    for k, (state, _, f, _) in enumerate(units):
        state[f] = current[k]


def kernel(
    fields, mixing, classes,
    outer, inner, east_halo, west_halo, north_halo, south_halo,
    outer_limits, inner_limits, matrices, weights, steps, north_send, south_send,
    load_sem, mix_sem, class_sem, send_sem, recv_sem,
):
    field_count, lons, lats, levels = fields.shape
    ops = mixing.shape[1]
    lon, lat = lax.axis_index("lon"), lax.axis_index("lat")
    lon_count, lat_count = lax.axis_size("lon"), lax.axis_size("lat")
    east = (lax.rem(lon + 1, lon_count), lat)
    west = (lax.rem(lon + lon_count - 1, lon_count), lat)
    north = (lon, lax.rem(lat + 1, lat_count))
    south = (lon, lax.rem(lat + lat_count - 1, lat_count))
    places = [(outer, 0), (inner, 0), (inner, lats), (outer, lats)]

    def load(chosen):
        copies = []
        for f in chosen:
            copies.append(pltpu.make_async_copy(mixing.at[f], matrices.at[f], mix_sem.at[f]))
            for i in (0, lons - 1, 1, 2):
                buffer, row = places[i]
                copies.append(pltpu.make_async_copy(
                    fields.at[f, i], buffer.at[f, pl.ds(row, lats)], load_sem.at[f * lons + i]
                ))
        for copy in copies:
            copy.start()
        return copies

    def prepare(chosen):
        for f in chosen:
            for o in range(ops):
                pieces = jnp.concatenate(split(matrices[f, o]), axis=0).T
                weights[f, o, pl.ds(0, levels), :] = pieces
                weights[f, o, pl.ds(levels, levels), :] = pieces
            outer[f, pl.ds(0, 2 * lats), :] = 0.5 * outer[f, pl.ds(0, 2 * lats), :]
            inner[f] = 0.5 * inner[f]
            outer[f, pl.ds(2 * lats, PAD), :] = jnp.concatenate(
                [inner[f, pl.ds(r, 1), :] for r in (0, lats - 1, lats, 2 * lats - 1)]
                + [jnp.zeros((PAD - 4, levels), jnp.float32)],
                axis=0,
            )

    class_copy = pltpu.make_async_copy(classes, steps, class_sem)
    class_copy.start()
    first, second = range(field_count // 2), range(field_count // 2, field_count)
    loads = load(first)

    barrier = pltpu.get_barrier_semaphore()
    for neighbour in (east, west, north, south):
        pl.semaphore_signal(barrier, inc=1, device_id=neighbour, device_id_type=MESH)

    class_copy.wait()
    edge_rows = []
    for i in range(lons):
        buffer, row = (outer_limits, places[i][1]) if i in (0, lons - 1) else (inner_limits, places[i][1])
        limit = jnp.broadcast_to(steps[pl.ds(i, 1), :] + 1, (levels, lats)).T
        buffer[pl.ds(row, lats), :] = limit
        if i in (1, 2):
            edge_rows += [limit[:1], limit[lats - 1:]]
    outer_limits[pl.ds(2 * lats, PAD), :] = jnp.concatenate(
        edge_rows + [jnp.zeros((PAD - 4, levels), jnp.int32)], axis=0
    )

    outers = [[outer, outer_limits, f, 0] for f in range(field_count)]
    inners = [[inner, inner_limits, f, 0] for f in range(field_count)]
    for copy in loads:
        copy.wait()
    loads = load(second)
    prepare(first)
    advance([outers[f] for f in first] + [inners[f] for f in first], HEAD, weights)
    for copy in loads:
        copy.wait()
    prepare(second)
    advance(outers, STEPS - HEAD, weights)

    pl.semaphore_wait(barrier, 4)
    copies = []

    def send(source, target, device):
        slot = len(copies)
        copy = pltpu.make_async_remote_copy(
            src_ref=source, dst_ref=target, send_sem=send_sem.at[slot], recv_sem=recv_sem.at[slot],
            device_id=device, device_id_type=MESH,
        )
        copy.start()
        copies.append(copy)

    def send_outer(chosen):
        for f in chosen:
            send(outer.at[f, pl.ds(lats, lats)], west_halo.at[f], east)
            send(outer.at[f, pl.ds(0, lats)], east_halo.at[f], west)

    send_outer(first)
    advance([outers[f] for f in second] + [inners[f] for f in second], HEAD, weights)
    send_outer(second)
    low_rows = (0, 2 * lats, 2 * lats + 2, lats)
    high_rows = (lats - 1, 2 * lats + 1, 2 * lats + 3, 2 * lats - 1)
    for f in range(field_count):
        for i in range(lons):
            south_send[pl.ds(f * lons + i, 1), :] = outer[f, pl.ds(low_rows[i], 1), :]
            north_send[pl.ds(f * lons + i, 1), :] = outer[f, pl.ds(high_rows[i], 1), :]
    send(north_send, south_halo, north)
    send(south_send, north_halo, south)

    advance(inners, STEPS - HEAD, weights)

    for copy in copies:
        copy.wait()


def smooth(outer, inner, east_halo, west_halo, north_halo, south_halo, out, result, out_sem):
    field_count, lons, lats, levels = out.shape
    lat, lat_count = lax.axis_index("lat"), lax.axis_size("lat")
    row = lax.broadcasted_iota(jnp.int32, (lats, levels), 0)
    stores = []
    for f in range(field_count):
        cells = [
            outer[f, pl.ds(0, lats), :],
            inner[f, pl.ds(0, lats), :],
            inner[f, pl.ds(lats, lats), :],
            outer[f, pl.ds(lats, lats), :],
        ]
        around = [west_halo[f]] + cells + [east_halo[f]]
        for i in range(lons):
            cell = cells[i]
            k = f * lons + i
            above = jnp.where(lat == lat_count - 1, cell[lats - 1:], north_halo[pl.ds(k, 1), :])
            below = jnp.where(lat == 0, cell[:1], south_halo[pl.ds(k, 1), :])
            northern = jnp.where(row == lats - 1, above, pltpu.roll(cell, lats - 1, 0))
            southern = jnp.where(row == 0, below, pltpu.roll(cell, 1, 0))
            result[f, i] = 0.4 * (cell + around[i] + around[i + 2] + northern + southern)
            copy = pltpu.make_async_copy(result.at[f, i], out.at[f, i], out_sem.at[k])
            copy.start()
            stores.append(copy)
    for copy in stores:
        copy.wait()


def per_device(fields, mixing, classes):
    field_count, lons, lats, levels = fields.shape
    ops = mixing.shape[1]
    f32, i32 = jnp.float32, jnp.int32
    halo = pltpu.VMEM((field_count, lats, levels), f32)
    edge = pltpu.VMEM((field_count * lons, levels), f32)
    copies = 2 + 2 * field_count
    rows = STEPS * ops * field_count * (lons * lats + PAD)
    in_hbm = pl.BlockSpec(memory_space=pltpu.HBM)
    in_vmem = pl.BlockSpec(memory_space=pltpu.VMEM)
    state = pl.pallas_call(
        kernel,
        out_shape=[
            pltpu.VMEM((field_count, 2 * lats + PAD, levels), f32),
            pltpu.VMEM((field_count, 2 * lats, levels), f32),
            halo, halo, edge, edge,
        ],
        in_specs=[in_hbm] * 3,
        out_specs=[in_vmem] * 6,
        scratch_shapes=[
            pltpu.VMEM((2 * lats + PAD, levels), i32),
            pltpu.VMEM((2 * lats, levels), i32),
            pltpu.VMEM(mixing.shape, f32),
            pltpu.VMEM((field_count, ops, 2 * levels, 2 * levels), jnp.bfloat16),
            pltpu.VMEM((lons, lats), i32),
            edge, edge,
            pltpu.SemaphoreType.DMA((field_count * lons,)),
            pltpu.SemaphoreType.DMA((field_count,)),
            pltpu.SemaphoreType.DMA,
            pltpu.SemaphoreType.DMA((copies,)),
            pltpu.SemaphoreType.DMA((copies,)),
        ],
        compiler_params=pltpu.CompilerParams(
            collective_id=0, has_side_effects=True, vmem_limit_bytes=32 * 2**20
        ),
        cost_estimate=pl.CostEstimate(
            flops=2 * rows * (2 * levels) ** 2, bytes_accessed=2 * 4 * fields.size, transcendentals=rows * levels
        ),
    )(*[pltpu.with_memory_space_constraint(x, pltpu.HBM) for x in (fields, mixing, classes)])
    return pl.pallas_call(
        smooth,
        out_shape=pltpu.HBM(fields.shape, f32),
        in_specs=[in_vmem] * 6,
        out_specs=in_hbm,
        scratch_shapes=[
            pltpu.VMEM(fields.shape, f32),
            pltpu.SemaphoreType.DMA((field_count * lons,)),
        ],
        compiler_params=pltpu.CompilerParams(vmem_limit_bytes=16 * 2**20),
        cost_estimate=pl.CostEstimate(flops=7 * fields.size, bytes_accessed=12 * fields.size, transcendentals=0),
    )(*state)


def solution(mesh):
    in_specs = (P(None, "lon", "lat", None), P(), P("lon", "lat"))
    out_specs = P(None, "lon", "lat", None)
    return jax.shard_map(
        per_device, mesh=mesh, in_specs=in_specs, out_specs=out_specs, check_vma=False
    )
```

time: 28.9 us -> 24.7 us (0.85)
  local copies, waits for them, and re-layouts: 4.1 us -> 0 us
    unnamed x7 -> x0, local copies, waits for them, and re-layouts: 4.1 us -> none
    pallas_call x1 -> x2, Pallas kernels: 24.6 us -> 24.5 us  [the longest x1 23.3 us: per_device(): pl.pallas_call(kernel, out_shape=[pltpu.VMEM((field_count, 2 * lats + PAD...]
where the time goes in v2:
time: 24.7 us; the launch traced here: 24.6 us
  Pallas kernels  24.5 us (99%)
    pallas_call x1, Pallas kernels, per_device(): pl.pallas_call(kernel, out_shape=[pltpu.VMEM((field_count, 2 * lats + PAD...  23.3 us
    pallas_call x1, Pallas kernels, per_device(): pl.pallas_call(smooth, out_shape=pltpu.HBM(fields.shape, f32), in_specs=[...  1.15 us

profile of v2, /device:TPU:1, one launch (start us, length us, event | category | flops | bytes accessed | tf_op | source)
XLA Modules:
  0.0 24.6 jit_solution(14237230589118440336)
XLA Ops:
  0.0 23.3 %shard_map.37 = (f32[4,272,128]{2,1,0:T(8,128)S(1)}, f32[4,256,128]{2,1,0:T(8,128)S(1)}, f32[4,128,128]{2,1,0:T(8,128)S(1)}, f32[4,128,128]{2,1,0:T(8,128)S(1)},...) custom-call(f32[4,4,128,128]{3,2,1,0:T(8,128)} %fields.1, f32[4,4,128,128]{3,2,1,0:T(8,128)} %mixing.1, s32[4,128]{1,0:T(4,128)} %classes.1), custom_call_target="tpu_custom_call" | custom-call | flops 17716740096 | bytes 2097152 | tf_op jit(solution)/shard_map/pallas_call | solution.py:188
  23.3 1.1 %shard_map.38 = f32[4,4,128,128]{3,2,1,0:T(8,128)} custom-call(f32[4,272,128]{2,1,0:T(8,128)S(1)} %get-tuple-element.11.outer, f32[4,256,128]{2,1,0:T(8,128)S(1)} %get-tuple-element.12.inner, f32[4,128,128]{2,1,0:T(8,128)S(1)} %get-tuple-element.13.east_halo, f32[4,128,128]{2,1,0:T(8,128)S(1)} %get-tuple-element.14.west_halo, ...), custom_call_target="tpu_custom_call" | custom-call | flops 1835008 | bytes 3145728 | tf_op jit(solution)/shard_map/pallas_call | solution.py:217

commit v3 on v2

v3 whole, which is shorter than its diff:
```python
import functools

import jax
import jax.numpy as jnp
from jax import lax
from jax.experimental import pallas as pl
from jax.experimental.pallas import tpu as pltpu
from jax.sharding import PartitionSpec as P

STEPS = 16
PAD = 16
MESH = pl.DeviceIdType.MESH


def stretches(field_count):
    left = {(i, f): STEPS for f in range(field_count) for i in (3, 0, 1, 2)}

    def stretch(count, always, shares, fill):
        shares, rounds = dict(shares), []
        for _ in range(count):
            units = [unit for unit in always if left[unit]]
            some = sorted((unit for unit in shares if shares[unit]), key=lambda unit: -shares[unit])
            units += some[:max(0, fill - len(units))]
            for unit in units:
                if unit in shares:
                    shares[unit] -= 1
            inner = sorted(
                (unit for unit in left if unit[0] in (1, 2) and left[unit] and unit not in units),
                key=lambda unit: -left[unit],
            )
            units += inner[:max(0, fill - len(units))]
            for unit in units:
                left[unit] -= 1
            rounds.append(units)
        return rounds

    def outer(*fields):
        return [(i, f) for f in fields for i in (3, 0)]

    def all_of(*fields):
        return [(i, f) for f in fields for i in (3, 0, 1, 2)]

    plan = [
        stretch(1, all_of(0), {}, 4)
        + stretch(1, outer(0, 1), {}, 7)
        + stretch(1, outer(0, 1, 2), {}, 7)
        + stretch(13, outer(0, 1), {(3, 2): 12, (3, 3): 13, (0, 2): 7, (0, 3): 7}, 7),
        stretch(1, outer(1, 2, 3), {}, 7),
        stretch(2, outer(2, 3), {}, 7),
        stretch(6, [(0, 2), (0, 3)], {}, 9),
        [],
    ]
    while any(left.values()):
        plan[-1] += stretch(1, [], {}, 8)
    return plan


def split(values):
    high = values.astype(jnp.bfloat16)
    low = (values - high.astype(jnp.float32)).astype(jnp.bfloat16)
    return high, low


def kernel(
    fields, mixing, classes,
    cells, east_halo, west_halo, north_halo, south_halo,
    limits, matrices, weights, steps, north_send, south_send,
    cell_sem, mix_sem, class_sem, send_sem, recv_sem,
):
    field_count, lons, lats, levels = fields.shape
    ops = mixing.shape[1]
    lon, lat = lax.axis_index("lon"), lax.axis_index("lat")
    lon_count, lat_count = lax.axis_size("lon"), lax.axis_size("lat")
    east = (lax.rem(lon + 1, lon_count), lat)
    west = (lax.rem(lon + lon_count - 1, lon_count), lat)
    north = (lon, lax.rem(lat + 1, lat_count))
    south = (lon, lax.rem(lat + lat_count - 1, lat_count))

    loads = []
    for f in range(field_count):
        loads += [
            pltpu.make_async_copy(mixing.at[f], matrices.at[f], mix_sem.at[f]),
            pltpu.make_async_copy(fields.at[f], cells.at[f], cell_sem.at[f]),
        ]
    loads.append(pltpu.make_async_copy(classes, steps, class_sem))
    for copy in loads:
        copy.start()

    barrier = pltpu.get_barrier_semaphore()
    for neighbour in (east, west, north, south):
        pl.semaphore_signal(barrier, inc=1, device_id=neighbour, device_id_type=MESH)

    for copy in loads:
        copy.wait()
    for i in range(lons):
        limits[i, pl.ds(0, lats), :] = jnp.broadcast_to(steps[pl.ds(i, 1), :] + 1, (levels, lats)).T
    limits[0, pl.ds(lats, PAD), :] = jnp.concatenate(
        [limits[i, pl.ds(row, 1), :] for row in (0, lats - 1) for i in (1, 2)]
        + [jnp.zeros((PAD - 4, levels), jnp.int32)],
        axis=0,
    )

    sends = []

    def send(source, target, device):
        slot = len(sends)
        copy = pltpu.make_async_remote_copy(
            src_ref=source, dst_ref=target, send_sem=send_sem.at[slot], recv_sem=recv_sem.at[slot],
            device_id=device, device_id_type=MESH,
        )
        sends.append(copy)
        return copy

    current, done = {}, {}

    def begin(f):
        for o in range(ops):
            pieces = jnp.concatenate(split(matrices[f, o]), axis=0).T
            weights[f, o, pl.ds(0, levels), :] = pieces
            weights[f, o, pl.ds(levels, levels), :] = pieces
        for i in range(lons):
            value = cells[f, i]
            if i == 0:
                value = jnp.concatenate(
                    [value]
                    + [cells[f, k, pl.ds(row, 1), :] for row in (0, lats - 1) for k in (1, 2)]
                    + [jnp.zeros((PAD - 4, levels), jnp.float32)],
                    axis=0,
                )
            current[i, f] = 0.5 * value
            done[i, f] = 0

    def finish(unit):
        i, f = unit
        value = current.pop(unit)
        cells[f, i] = value[:lats]
        if i == 0:
            for k in (1, 2):
                south_send[pl.ds(f * lons + k, 1), :] = value[lats + k - 1:lats + k]
                north_send[pl.ds(f * lons + k, 1), :] = value[lats + k + 1:lats + k + 2]
        if i in (0, 3):
            south_send[pl.ds(f * lons + i, 1), :] = value[:1]
            north_send[pl.ds(f * lons + i, 1), :] = value[lats - 1:lats]

    def step(units):
        pairs = {}
        for unit in units:
            pairs.setdefault((unit[0] in (1, 2), unit[1]), []).append(unit)
        values = {key: jnp.concatenate([current[unit] for unit in pair], axis=0) for key, pair in pairs.items()}
        for o in range(ops):
            for key in pairs:
                pieces = jnp.concatenate(split(values[key]), axis=1)
                mixed = jnp.dot(pieces, weights[key[1], o], preferred_element_type=jnp.float32)
                values[key] = jnp.tanh(mixed[:, :levels] + mixed[:, levels:])
        for key, pair in pairs.items():
            row = 0
            for unit in pair:
                height = current[unit].shape[0]
                active = limits[unit[0], pl.ds(0, height), :] > done[unit]
                current[unit] = jnp.where(active, values[key][row:row + height], current[unit])
                row += height
                done[unit] += 1

    edges, sent = [], {0: 0, 3: 0}
    for stretch in stretches(field_count):
        for units in stretch:
            for unit in units:
                if unit not in done:
                    begin(unit[1])
            step(units)
        over = [unit for unit in current if done[unit] == STEPS]
        for unit in over:
            finish(unit)
        if over and not sends:
            pl.semaphore_wait(barrier, 4)
        for i, halo, device in ((3, west_halo, east), (0, east_halo, west)):
            found = sorted(f for k, f in over if k == i)
            if found:
                chosen = pl.ds(found[0], len(found))
                send(cells.at[chosen, i], halo.at[chosen], device).start()
                sent[i] += len(found)
        if sent == {0: field_count, 3: field_count} and not edges:
            edges += [send(north_send, south_halo, north), send(south_send, north_halo, south)]

            @pl.when(lat < lat_count - 1)
            def _():
                edges[0].start()

            @pl.when(lat > 0)
            def _():
                edges[1].start()

    for copy in sends[:-2]:
        copy.wait()

    @pl.when(lat < lat_count - 1)
    def _():
        edges[0].wait_send()
        edges[1].wait_recv()

    @pl.when(lat > 0)
    def _():
        edges[1].wait_send()
        edges[0].wait_recv()


def smooth(cells, east_halo, west_halo, north_halo, south_halo, out, result, out_sem):
    field_count, lons, lats, levels = out.shape
    lat, lat_count = lax.axis_index("lat"), lax.axis_size("lat")
    row = lax.broadcasted_iota(jnp.int32, (lats, levels), 0)
    stores = []
    for f in range(field_count):
        field = [cells[f, i] for i in range(lons)]
        around = [west_halo[f]] + field + [east_halo[f]]
        for i in range(lons):
            cell = field[i]
            k = f * lons + i
            above = jnp.where(lat == lat_count - 1, cell[lats - 1:], north_halo[pl.ds(k, 1), :])
            below = jnp.where(lat == 0, cell[:1], south_halo[pl.ds(k, 1), :])
            northern = jnp.where(row == lats - 1, above, pltpu.roll(cell, lats - 1, 0))
            southern = jnp.where(row == 0, below, pltpu.roll(cell, 1, 0))
            result[f, i] = 0.4 * (cell + around[i] + around[i + 2] + northern + southern)
            copy = pltpu.make_async_copy(result.at[f, i], out.at[f, i], out_sem.at[k])
            copy.start()
            stores.append(copy)
    for copy in stores:
        copy.wait()


def per_device(fields, mixing, classes):
    field_count, lons, lats, levels = fields.shape
    ops = mixing.shape[1]
    f32, i32 = jnp.float32, jnp.int32
    halo = pltpu.VMEM((field_count, lats, levels), f32)
    edge = pltpu.VMEM((field_count * lons, levels), f32)
    copies = 2 + 2 * field_count
    rows = STEPS * ops * field_count * (lons * lats + PAD)
    in_hbm = pl.BlockSpec(memory_space=pltpu.HBM)
    in_vmem = pl.BlockSpec(memory_space=pltpu.VMEM)
    state = pl.pallas_call(
        kernel,
        out_shape=[pltpu.VMEM(fields.shape, f32), halo, halo, edge, edge],
        in_specs=[in_hbm] * 3,
        out_specs=[in_vmem] * 5,
        scratch_shapes=[
            pltpu.VMEM((lons, lats + PAD, levels), i32),
            pltpu.VMEM(mixing.shape, f32),
            pltpu.VMEM((field_count, ops, 2 * levels, 2 * levels), jnp.bfloat16),
            pltpu.VMEM((lons, lats), i32),
            edge, edge,
            pltpu.SemaphoreType.DMA((field_count,)),
            pltpu.SemaphoreType.DMA((field_count,)),
            pltpu.SemaphoreType.DMA,
            pltpu.SemaphoreType.DMA((copies,)),
            pltpu.SemaphoreType.DMA((copies,)),
        ],
        compiler_params=pltpu.CompilerParams(
            collective_id=0, has_side_effects=True, vmem_limit_bytes=32 * 2**20
        ),
        cost_estimate=pl.CostEstimate(
            flops=2 * rows * (2 * levels) ** 2, bytes_accessed=2 * 4 * fields.size, transcendentals=rows * levels
        ),
    )(*[pltpu.with_memory_space_constraint(x, pltpu.HBM) for x in (fields, mixing, classes)])
    return pl.pallas_call(
        smooth,
        out_shape=pltpu.HBM(fields.shape, f32),
        in_specs=[in_vmem] * 5,
        out_specs=in_hbm,
        scratch_shapes=[
            pltpu.VMEM(fields.shape, f32),
            pltpu.SemaphoreType.DMA((field_count * lons,)),
        ],
        compiler_params=pltpu.CompilerParams(vmem_limit_bytes=16 * 2**20),
        cost_estimate=pl.CostEstimate(flops=7 * fields.size, bytes_accessed=12 * fields.size, transcendentals=0),
    )(*state)


def solution(mesh):
    in_specs = (P(None, "lon", "lat", None), P(), P("lon", "lat"))
    out_specs = P(None, "lon", "lat", None)
    return jax.shard_map(
        per_device, mesh=mesh, in_specs=in_specs, out_specs=out_specs, check_vma=False
    )
```

time: 24.7 us -> 23.8 us (0.964)
  Pallas kernels: 24.5 us -> 23.5 us
    pallas_call x1, Pallas kernels: 23.3 us -> 22.4 us  [per_device(): pl.pallas_call(kernel, out_shape=[pltpu.VMEM(fields.shape, f32), halo, ha...]
where the time goes in v3:
time: 23.8 us; the launch traced here: 23.7 us
  Pallas kernels  23.5 us (99%)
    pallas_call x1, Pallas kernels, per_device(): pl.pallas_call(kernel, out_shape=[pltpu.VMEM(fields.shape, f32), halo, ha...  22.4 us
    pallas_call x1, Pallas kernels, per_device(): pl.pallas_call(smooth, out_shape=pltpu.HBM(fields.shape, f32), in_specs=[...  1.15 us

profile of v3, /device:TPU:1, one launch (start us, length us, event | category | flops | bytes accessed | tf_op | source)
XLA Modules:
  0.0 23.7 jit_solution(9273855449598710290)
XLA Ops:
  0.0 22.4 %shard_map.37 = (f32[4,4,128,128]{3,2,1,0:T(8,128)S(1)}, f32[4,128,128]{2,1,0:T(8,128)S(1)}, f32[4,128,128]{2,1,0:T(8,128)S(1)}, f32[16,128]{1,0:T(8,128)S(1)}, f32[16,128]{1,0:T(8,128)S(1)}) custom-call(f32[4,4,128,128]{3,2,1,0:T(8,128)} %fields.1, f32[4,4,128,128]{3,2,1,0:T(8,128)} %mixing.1, s32[4,128]{1,0:T(4,128)} %classes.1), custom_call_target="tpu_custom_call" | custom-call | flops 17716740096 | bytes 2097152 | tf_op jit(solution)/shard_map/pallas_call | solution.py:240
  22.4 1.1 %shard_map.38 = f32[4,4,128,128]{3,2,1,0:T(8,128)} custom-call(f32[4,4,128,128]{3,2,1,0:T(8,128)S(1)} %get-tuple-element.10.cells, f32[4,128,128]{2,1,0:T(8,128)S(1)} %get-tuple-element.11.east_halo, f32[4,128,128]{2,1,0:T(8,128)S(1)} %get-tuple-element.12.west_halo, f32[16,128]{1,0:T(8,128)S(1)} %get-tuple-element.13.north_halo, ...), custom_call_target="tpu_custom_call" | custom-call | flops 1835008 | bytes 3145728 | tf_op jit(solution)/shard_map/pallas_call | solution.py:264

commit v4 on v3

--- a/solution.py
+++ b/solution.py
@@ -63,8 +63,8 @@
 
 def kernel(
     fields, mixing, classes,
-    cells, east_halo, west_halo, north_halo, south_halo,
-    limits, matrices, weights, steps, north_send, south_send,
+    partial, east_halo, west_halo, north_halo, south_halo,
+    cells, limits, matrices, weights, steps, north_send, south_send,
     cell_sem, mix_sem, class_sem, send_sem, recv_sem,
 ):
     field_count, lons, lats, levels = fields.shape
@@ -190,6 +190,26 @@
             def _():
                 edges[1].start()
 
+    row = lax.broadcasted_iota(jnp.int32, (lats, levels), 0)
+    for f in range(field_count):
+        field = [cells[f, i] for i in range(lons)]
+        for i in range(lons):
+            northern = jnp.where(row == lats - 1, 0.0, pltpu.roll(field[i], lats - 1, 0))
+            southern = jnp.where(row == 0, 0.0, pltpu.roll(field[i], 1, 0))
+            total = field[i] + northern + southern
+            for k in (i - 1, i + 1):
+                if 0 <= k < lons:
+                    total = total + field[k]
+            partial[f, i] = 0.4 * total
+
+    @pl.when(lat == lat_count - 1)
+    def _():
+        north_halo[...] = north_send[...]
+
+    @pl.when(lat == 0)
+    def _():
+        south_halo[...] = south_send[...]
+
     for copy in sends[:-2]:
         copy.wait()
 
@@ -204,22 +224,20 @@
         edges[0].wait_recv()
 
 
-def smooth(cells, east_halo, west_halo, north_halo, south_halo, out, result, out_sem):
+def smooth(partial, east_halo, west_halo, north_halo, south_halo, out, result, out_sem):
     field_count, lons, lats, levels = out.shape
-    lat, lat_count = lax.axis_index("lat"), lax.axis_size("lat")
-    row = lax.broadcasted_iota(jnp.int32, (lats, levels), 0)
     stores = []
     for f in range(field_count):
-        field = [cells[f, i] for i in range(lons)]
-        around = [west_halo[f]] + field + [east_halo[f]]
         for i in range(lons):
-            cell = field[i]
             k = f * lons + i
-            above = jnp.where(lat == lat_count - 1, cell[lats - 1:], north_halo[pl.ds(k, 1), :])
-            below = jnp.where(lat == 0, cell[:1], south_halo[pl.ds(k, 1), :])
-            northern = jnp.where(row == lats - 1, above, pltpu.roll(cell, lats - 1, 0))
-            southern = jnp.where(row == 0, below, pltpu.roll(cell, 1, 0))
-            result[f, i] = 0.4 * (cell + around[i] + around[i + 2] + northern + southern)
+            total = partial[f, i]
+            if i == 0:
+                total = total + 0.4 * west_halo[f]
+            if i == lons - 1:
+                total = total + 0.4 * east_halo[f]
+            result[f, i] = total
+            result[f, i, pl.ds(0, 1), :] = total[:1] + 0.4 * south_halo[pl.ds(k, 1), :]
+            result[f, i, pl.ds(lats - 1, 1), :] = total[lats - 1:] + 0.4 * north_halo[pl.ds(k, 1), :]
             copy = pltpu.make_async_copy(result.at[f, i], out.at[f, i], out_sem.at[k])
             copy.start()
             stores.append(copy)
@@ -243,6 +261,7 @@
         in_specs=[in_hbm] * 3,
         out_specs=[in_vmem] * 5,
         scratch_shapes=[
+            pltpu.VMEM(fields.shape, f32),
             pltpu.VMEM((lons, lats + PAD, levels), i32),
             pltpu.VMEM(mixing.shape, f32),
             pltpu.VMEM((field_count, ops, 2 * levels, 2 * levels), jnp.bfloat16),

time: 23.8 us -> 23.7 us (level)
  no operation moved by 1% of the time
where the time goes in v4:
time: 23.7 us; the launch traced here: 23.6 us
  Pallas kernels  23.4 us (99%)
    pallas_call x1, Pallas kernels, per_device(): pl.pallas_call(kernel, out_shape=[pltpu.VMEM(fields.shape, f32), halo, ha...  22.3 us
    pallas_call x1, Pallas kernels, per_device(): pl.pallas_call(smooth, out_shape=pltpu.HBM(fields.shape, f32), in_specs=[...  1.1 us

profile of v4, /device:TPU:1, one launch (start us, length us, event | category | flops | bytes accessed | tf_op | source)
XLA Modules:
  0.0 23.6 jit_solution(6651872915526705245)
XLA Ops:
  0.0 22.3 %shard_map.37 = (f32[4,4,128,128]{3,2,1,0:T(8,128)S(1)}, f32[4,128,128]{2,1,0:T(8,128)S(1)}, f32[4,128,128]{2,1,0:T(8,128)S(1)}, f32[16,128]{1,0:T(8,128)S(1)}, f32[16,128]{1,0:T(8,128)S(1)}) custom-call(f32[4,4,128,128]{3,2,1,0:T(8,128)} %fields.1, f32[4,4,128,128]{3,2,1,0:T(8,128)} %mixing.1, s32[4,128]{1,0:T(4,128)} %classes.1), custom_call_target="tpu_custom_call" | custom-call | flops 17716740096 | bytes 2097152 | tf_op jit(solution)/shard_map/pallas_call | solution.py:258
  22.4 1.1 %shard_map.38 = f32[4,4,128,128]{3,2,1,0:T(8,128)} custom-call(f32[4,4,128,128]{3,2,1,0:T(8,128)S(1)} %get-tuple-element.10.partial, f32[4,128,128]{2,1,0:T(8,128)S(1)} %get-tuple-element.11.east_halo, f32[4,128,128]{2,1,0:T(8,128)S(1)} %get-tuple-element.12.west_halo, f32[16,128]{1,0:T(8,128)S(1)} %get-tuple-element.13.north_halo, ...), custom_call_target="tpu_custom_call" | custom-call | flops 1835008 | bytes 3145728 | tf_op jit(solution)/shard_map/pallas_call | solution.py:283
